TPU v7x, 32 devices: a whole 2x2x4 slice. The times are simulated.
32 devices in a mesh: grp: 4 (over y, core), ctx: 8 (over z, x).
Axes of the slice: x: 2, y: 2, z: 4, core: 2. Of those that a mesh axis runs over, the one named last changes fastest.
Arguments:
- query_rows: bfloat16 [4, 1024, 4096], P('grp', 'ctx'), may hold values from -6 to 6
- key_rows: bfloat16 [4, 1024, 512], P('grp', 'ctx'), may hold values from -6 to 6
- value_rows: bfloat16 [4, 1024, 512], P('grp', 'ctx'), may hold values from -5 to 5
- output_rows: bfloat16 [4, 1024, 4096], P('grp', 'ctx'), may hold values from -4 to 4
- output_grad: bfloat16 [4, 1024, 4096], P('grp', 'ctx'), may hold values from -5 to 5
- loss_mask: int32 [4, 1024], P('grp', 'ctx'), may hold values from 0 to 1
- doc_lengths: int32 [4, 12], P('grp'), may hold values from 1 to 256, 1024 in all within a row
- balance_plan: int32 [4, 128], P('grp'), may hold values from 0 to 127, as said below
Outputs:
- query_grad: bfloat16 [4, 1024, 4096], P('grp', 'ctx')
- key_grad: bfloat16 [4, 1024, 512], P('grp', 'ctx')
- value_grad: bfloat16 [4, 1024, 512], P('grp', 'ctx')
Inputs may be any that keep to these rules, and one draw needn't show every extreme that they name: Each row is a permutation of 0 to 127. Span c of a sequence (its tokens c * 8 to c * 8 + 7) goes to index balance_plan // 16 of ctx; of the 16 spans of one index of ctx at most 2 go to the same index.
All inputs are finite; a program needn't handle non-finite values.
Results may differ from a plain program's by a relative error of at most 0.0051.
Values may be sent and summed in bfloat16 or wider, within the bound.
A program may use at most 128 MiB of HBM per device.

v0:
```python
import jax
import jax.numpy as jnp
from jax import lax
from jax.sharding import PartitionSpec as P

HD = 128
QH = 32
KVH = 4
SPAN = 8
NEGATIVE = -1e30


def key_block():
    return 512


def doc_index(positions, doc_ends):
    return jnp.sum((positions[:, None] >= doc_ends[None, :]).astype(jnp.int32), axis=1)


def visible(query_pos, query_doc, key_pos, doc_ends):
    key_doc = doc_index(key_pos, doc_ends)
    return (key_pos[None, :] <= query_pos[:, None]) & (key_doc[None, :] == query_doc[:, None])


def head_scores(q_heads, k_heads, scale_value):
    return (
        jnp.einsum("rgsd,ngd->gsrn", q_heads, k_heads, preferred_element_type=jnp.float32)
        * scale_value
    )


def over_blocks(function, folded, members):
    row_total = members[0].shape[0]
    block_rows = key_block()
    step_count = row_total // block_rows
    stacked = tuple(
        (member.reshape((step_count, block_rows) + member.shape[1:]) for member in members)
    )

    def advance(carried, scanned):
        block_index, pieces = scanned
        positions = block_index * block_rows + jnp.arange(block_rows, dtype=jnp.int32)
        return (function(carried, pieces, positions), None)

    result, unused = lax.scan(advance, folded, (jnp.arange(step_count, dtype=jnp.int32), stacked))
    return result


def stats_update(carried, k_heads, key_pos, context):
    q_heads, query_pos, query_doc, doc_ends, scale_value = context
    old_peak, running_sum = carried
    scores = head_scores(q_heads, k_heads, scale_value)
    visible_mask = visible(query_pos, query_doc, key_pos, doc_ends)
    scores = jnp.where(visible_mask, scores, NEGATIVE)
    new_peak = jnp.maximum(old_peak, jnp.max(scores, axis=-1))
    weights = jnp.where(visible_mask, jnp.exp(scores - new_peak[..., None]), 0.0)
    running_sum = running_sum * jnp.exp(old_peak - new_peak) + jnp.sum(weights, axis=-1)
    return (new_peak, running_sum)


def block_grads(context, k_heads, v_heads, key_pos):
    q_heads, g_heads, query_pos, query_doc, doc_ends, lse_rows, delta_heads, scale_value = context
    scores = head_scores(q_heads, k_heads, scale_value)
    visible_mask = visible(query_pos, query_doc, key_pos, doc_ends)
    probs_full = jnp.where(
        visible_mask, jnp.exp(jnp.where(visible_mask, scores - lse_rows[..., None], NEGATIVE)), 0.0
    )
    probs_half = probs_full.astype(jnp.bfloat16)
    dprobs = jnp.einsum("rgsd,ngd->gsrn", g_heads, v_heads, preferred_element_type=jnp.float32)
    dscores = (probs_full * (dprobs - delta_heads[..., None]) * scale_value).astype(jnp.bfloat16)
    query_part = jnp.einsum("gsrn,ngd->rgsd", dscores, k_heads, preferred_element_type=jnp.float32)
    key_part = jnp.einsum("gsrn,rgsd->ngd", dscores, q_heads, preferred_element_type=jnp.float32)
    value_part = jnp.einsum(
        "gsrn,rgsd->ngd", probs_half, g_heads, preferred_element_type=jnp.float32
    )
    return (query_part, key_part, value_part)


def row_delta(grad_local, output_local):
    local_rows = grad_local.shape[0]
    product = grad_local.astype(jnp.float32) * output_local.astype(jnp.float32)
    return jnp.sum(product.reshape(local_rows, QH, HD), axis=-1)


def shards(
    query_rows, key_rows, value_rows, output_rows, output_grad, loss_mask, doc_lengths, balance_plan
):
    devices = lax.axis_size("ctx")
    device = lax.axis_index("ctx")
    local_rows = query_rows.shape[1]
    per_device = local_rows // SPAN
    slot_count = (per_device + devices - 1) // devices
    group_size = QH // KVH
    scale_value = HD ** (-0.5)
    counted = jnp.sum(loss_mask.astype(jnp.float32))
    total_counted = lax.psum(counted, ("grp", "ctx"))
    factor = lax.axis_size("grp") * devices * local_rows / jnp.maximum(total_counted, 1.0)
    grad_masked = output_grad[0] * loss_mask[0][:, None].astype(jnp.bfloat16)
    plan_row = balance_plan[0]
    dest_all = plan_row // per_device
    dest_grid = dest_all.reshape(devices, per_device)
    earlier = jnp.arange(per_device)[None, :] < jnp.arange(per_device)[:, None]
    same_dest = dest_grid[:, :, None] == dest_grid[:, None, :]
    rank_all = jnp.sum((same_dest & earlier[None, :, :]).astype(jnp.int32), axis=2).reshape(-1)
    inverse = jnp.argsort(plan_row)
    handled = lax.dynamic_slice_in_dim(inverse, device * per_device, per_device)
    receive_index = handled // per_device * slot_count + jnp.take(rank_all, handled)
    send_dest = lax.dynamic_slice_in_dim(dest_all, device * per_device, per_device)
    send_rank = lax.dynamic_slice_in_dim(rank_all, device * per_device, per_device)
    send_index = send_dest * slot_count + send_rank

    def pack_rows(member):
        row_width = member.shape[-1]
        pieces = member.reshape(per_device, SPAN, row_width)
        buffer = jnp.zeros((devices * slot_count, SPAN, row_width), member.dtype)
        return buffer.at[send_index].set(pieces)

    def unpack(member):
        return jnp.take(member, receive_index, axis=0).reshape(local_rows, member.shape[-1])

    moved_query, moved_grad, moved_output = (
        lax.all_to_all(pack_rows(query_rows[0]), "ctx", split_axis=0, concat_axis=0, tiled=True),
        lax.all_to_all(pack_rows(grad_masked), "ctx", split_axis=0, concat_axis=0, tiled=True),
        lax.all_to_all(pack_rows(output_rows[0]), "ctx", split_axis=0, concat_axis=0, tiled=True),
    )
    delta_rows = row_delta(unpack(moved_grad), unpack(moved_output))
    q_local = unpack(moved_query)
    g_local = unpack(moved_grad)
    q_heads = q_local.reshape(local_rows, KVH, group_size, HD)
    g_heads = g_local.reshape(local_rows, KVH, group_size, HD)
    delta_heads = jnp.transpose(delta_rows).reshape(KVH, group_size, local_rows)
    query_pos = (handled[:, None] * SPAN + jnp.arange(SPAN, dtype=jnp.int32)[None, :]).reshape(
        local_rows
    )
    doc_ends = jnp.cumsum(doc_lengths[0])
    query_doc = doc_index(query_pos, doc_ends)
    stats_context = (q_heads, query_pos, query_doc, doc_ends, scale_value)
    stats_initial = (
        jnp.full((KVH, group_size, local_rows), NEGATIVE, jnp.float32),
        jnp.zeros((KVH, group_size, local_rows), jnp.float32),
    )

    def stats_step_rows(carried, members, positions):
        return stats_update(carried, members[0].reshape(-1, KVH, HD), positions, stats_context)

    peak_rows, sum_rows = over_blocks(
        stats_step_rows, stats_initial, (lax.all_gather(key_rows, "ctx", axis=1, tiled=True)[0],)
    )
    lse_rows = peak_rows + jnp.log(sum_rows)
    grad_context = (
        q_heads,
        g_heads,
        query_pos,
        query_doc,
        doc_ends,
        lse_rows,
        delta_heads,
        scale_value,
    )
    dq_zero = jnp.zeros((local_rows, KVH, group_size, HD), jnp.float32)
    seq_total = local_rows * devices
    grads_initial = (
        dq_zero,
        jnp.zeros((seq_total, KVH, HD), jnp.float32),
        jnp.zeros((seq_total, KVH, HD), jnp.float32),
    )

    def grads_step_rows(carried, members, positions):
        dq_acc, dk_all, dv_all = carried
        k_heads = members[0].reshape(-1, KVH, HD)
        v_heads = members[1].reshape(-1, KVH, HD)
        query_part, key_part, value_part = block_grads(grad_context, k_heads, v_heads, positions)
        first_row = positions[0]
        old_keys = lax.dynamic_slice_in_dim(dk_all, first_row, key_part.shape[0], 0)
        dk_all = lax.dynamic_update_slice_in_dim(dk_all, old_keys + key_part, first_row, 0)
        old_values = lax.dynamic_slice_in_dim(dv_all, first_row, value_part.shape[0], 0)
        dv_all = lax.dynamic_update_slice_in_dim(dv_all, old_values + value_part, first_row, 0)
        return (dq_acc + query_part, dk_all, dv_all)

    dq_sum, dk_all, dv_all = over_blocks(
        grads_step_rows,
        grads_initial,
        (
            lax.all_gather(key_rows, "ctx", axis=1, tiled=True)[0],
            lax.all_gather(value_rows, "ctx", axis=1, tiled=True)[0],
        ),
    )
    dk_mine, dv_mine = (
        lax.psum_scatter(dk_all, "ctx", scatter_dimension=0, tiled=True),
        lax.psum_scatter(dv_all, "ctx", scatter_dimension=0, tiled=True),
    )
    query_grad = (dq_sum * factor).astype(jnp.bfloat16).reshape(1, local_rows, QH * HD)
    key_grad = (dk_mine * factor).astype(jnp.bfloat16).reshape(1, local_rows, KVH * HD)
    value_grad = (dv_mine * factor).astype(jnp.bfloat16).reshape(1, local_rows, KVH * HD)
    return (query_grad, key_grad, value_grad)


def solution(mesh):
    in_specs = (
        P("grp", "ctx", None),
        P("grp", "ctx", None),
        P("grp", "ctx", None),
        P("grp", "ctx", None),
        P("grp", "ctx", None),
        P("grp", "ctx"),
        P("grp", None),
        P("grp", None),
    )
    out_specs = (P("grp", "ctx", None), P("grp", "ctx", None), P("grp", "ctx", None))
    return jax.shard_map(shards, mesh=mesh, in_specs=in_specs, out_specs=out_specs, check_vma=False)
```

profile of v0, /device:TPU:0, one launch (start us, length us, event | category | flops | bytes accessed | tf_op | source)
XLA Modules:
  0.0 347.5 jit_solution(4692239312249407797)
XLA Ops:
  11.4 3.4 scatter_fusion
  14.8 7.2 %all-to-all-start = ((bf16[16,8,4096]{2,1,0:T(8,128)(2,1)}), bf16[16,8,4096]{2,1,0:T(8,128)(2,1)S(1)}, u32[]{:S(2)}, u32[]{:S(2)}) async-start(bf16[16,8,4096]{2,1,0:T(8,128)(2,1)} %scatter_fusion), calls=%async_computation | async-start | bytes 2097152 | tf_op jit(solution)/shard_map/all_to_all | solution.py:123
  26.0 2.9 scatter_fusion.1
  29.0 23.0 %all-to-all-done = bf16[16,8,4096]{2,1,0:T(8,128)(2,1)S(1)} async-done(((bf16[16,8,4096]{2,1,0:T(8,128)(2,1)}), bf16[16,8,4096]{2,1,0:T(8,128)(2,1)S(1)}, u32[]{:S(2)}, u32[]{:S(2)}) %all-to-all-start) | async-done | bytes 1048608 | tf_op jit(solution)/shard_map/all_to_all | solution.py:123
  52.0 4.2 %all-to-all-start.1 = ((bf16[16,8,4096]{2,1,0:T(8,128)(2,1)}), bf16[16,8,4096]{2,1,0:T(8,128)(2,1)}, u32[]{:S(2)}, u32[]{:S(2)}) async-start(bf16[16,8,4096]{2,1,0:T(8,128)(2,1)} %scatter_fusion.1), calls=%async_computation.1 | async-start | bytes 2097152 | tf_op jit(solution)/shard_map/all_to_all | solution.py:124
  57.2 2.5 sort.17
  61.8 3.4 scatter_fusion.2
  65.4 21.0 %all-gather.3.cloned.1.call-done = bf16[1,1024,512]{2,1,0:T(8,128)(2,1)} async-done(((bf16[1,128,512]{2,1,0:T(8,128)(2,1)}), bf16[1,1024,512]{2,1,0:T(8,128)(2,1)}) %all-gather.3.cloned.1.call-update) | async-done | bytes 1048592 | tf_op jit(solution)/shard_map/all_gather | solution.py:185
  90.1 4.2 %all-to-all-start.2 = ((bf16[16,8,4096]{2,1,0:T(8,128)(2,1)}), bf16[16,8,4096]{2,1,0:T(8,128)(2,1)}, u32[]{:S(2)}, u32[]{:S(2)}) async-start(bf16[16,8,4096]{2,1,0:T(8,128)(2,1)} %scatter_fusion.2), calls=%async_computation.2 | async-start | bytes 2097152 | tf_op jit(solution)/shard_map/all_to_all | solution.py:125
  94.4 1.8 gather_fusion.2
  98.1 10.8 %while.28 = (s32[]{:T(128)}, f32[4,8,128]{2,1,0:T(8,128)S(1)}, f32[4,8,128]{2,1,0:T(8,128)S(1)}, s32[2]{0:T(128)S(1)}, s32[12]{0:T(128)S(1)}, /*index=5*/s32[128...) while((s32[]{:T(128)}, f32[4,8,128]{2,1,0:T(8,128)S(1)}, ...), condition=%wide.region_9.11_spmd.clone, body=%wide.region_5.10_spmd.clone.sunk | while | flops 553883776 | bytes 19821336 | solution.py:46
  101.3 2.1 select_reduce_fusion.2
  106.7 2.1 select_reduce_fusion.2
  111.7 17.6 %all-to-all-done.2 = bf16[16,8,4096]{2,1,0:T(8,128)(2,1)} async-done(((bf16[16,8,4096]{2,1,0:T(8,128)(2,1)}), bf16[16,8,4096]{2,1,0:T(8,128)(2,1)}, u32[]{:S(2)}, u32[]{:S(2)}) %all-to-all-start.2) | async-done | bytes 1048608 | tf_op jit(solution)/shard_map/all_to_all | solution.py:125
  129.3 2.8 gather_fusion.3
  133.8 1.7 copy.84
  135.5 2.2 reduce_sum.65
  140.7 59.4 %while.29 = (s32[]{:T(128)}, f32[128,4,8,128]{0,3,2,1:T(8,128)}, f32[1024,4,128]{2,0,1:T(8,128)}, f32[1024,4,128]{2,0,1:T(8,128)}, bf16[2,512,512]{1,2,0:T(8,128...) while((s32[]{:T(128)}, f32[128,4,8,128]{0,3,2,1:T(8,128)}, ...), condition=%wide.region_15.17_spmd.clone, body=%wide.region_13.16_spmd.clone.sunk | while | flops 2713405440 | bytes 80475096 | solution.py:46
  148.0 3.1 fusion.77
  151.1 3.5 %fusion.75 = bf16[4,8,128,512]{2,3,1,0:T(8,128)(2,1)S(1)} fusion(f32[4,512,128,8]{2,1,3,0:T(8,128)S(1)} %fusion.74, f32[4,8,128]{2,1,0:T(8,128)S(1)} %bitcast.176, f32[4,8,128]{2,1,0:T(8,128)S(1)} %get-tuple-element.587, pred[128,512]{0,1:T(8,128)(4,1)S(1)} %compare_and_fusion.6, bf16[512,4,128,1]{0,2,3,1:T(8,128)(2,1)S(1)} %bitcast.164, ...), kind=kOutput, calls=%fused_computation.23.clone.1 | convolution fusion | flops 553648128 | bytes 14254080 | tf_op jit(solution)/shard_map/while/body/eval_jaxpr/rgsd,ngd->gsrn/dot_general | solution.py:70
  156.0 2.3 bitcast_add_fusion.2
  158.2 5.9 %dynamic_update_slice.10 = f32[1024,4,128]{2,0,1:T(8,128)} dynamic-update-slice(f32[1024,4,128]{2,0,1:T(8,128)} %get-tuple-element.562, f32[512,4,128]{2,0,1:T(8,128)S(1)} %fusion.76, s32[]{:T(128)S(6)} %select_n.158, s32[]{:T(128)} %constant.75.clone.1..sunk.1, s32[]{:T(128)} %constant.75.clone.1..sunk.1) | dynamic-update-slice | bytes 2097156 | tf_op jit(solution)/shard_map/while/body/eval_jaxpr/dynamic_update_slice | solution.py:176
  164.1 6.2 %dynamic_update_slice.11 = f32[1024,4,128]{2,0,1:T(8,128)} dynamic-update-slice(f32[1024,4,128]{2,0,1:T(8,128)} %get-tuple-element.563, f32[512,4,128]{2,0,1:T(8,128)} %fusion.77, s32[]{:T(128)S(6)} %select_n.158, s32[]{:T(128)} %constant.75.clone.1..sunk.1, s32[]{:T(128)} %constant.75.clone.1..sunk.1) | dynamic-update-slice | bytes 2097156 | tf_op jit(solution)/shard_map/while/body/eval_jaxpr/dynamic_update_slice | solution.py:178
  177.7 3.1 fusion.77
  180.7 3.5 %fusion.75 = bf16[4,8,128,512]{2,3,1,0:T(8,128)(2,1)S(1)} fusion(f32[4,512,128,8]{2,1,3,0:T(8,128)S(1)} %fusion.74, f32[4,8,128]{2,1,0:T(8,128)S(1)} %bitcast.176, f32[4,8,128]{2,1,0:T(8,128)S(1)} %get-tuple-element.587, pred[128,512]{0,1:T(8,128)(4,1)S(1)} %compare_and_fusion.6, bf16[512,4,128,1]{0,2,3,1:T(8,128)(2,1)S(1)} %bitcast.164, ...), kind=kOutput, calls=%fused_computation.23.clone.1 | convolution fusion | flops 553648128 | bytes 14254080 | tf_op jit(solution)/shard_map/while/body/eval_jaxpr/rgsd,ngd->gsrn/dot_general | solution.py:70
  185.6 3.9 %bitcast_add_fusion.2 = f32[128,4,8,128]{0,3,2,1:T(8,128)} fusion(f32[128,4,8,128]{0,3,2,1:T(8,128)} %get-tuple-element.561, bf16[512,4,128,1]{0,2,3,1:T(8,128)(2,1)S(1)} %bitcast.162, bf16[4,8,128,512]{2,3,1,0:T(8,128)(2,1)S(1)} %fusion.75, pred[]{:T(512)S(6)} %compare.25), kind=kOutput, calls=%fused_computation.31.clone.1 | convolution fusion | flops 537919488 | bytes 8912897 | tf_op jit(solution)/shard_map/while/body/eval_jaxpr/gsrn,ngd->rgsd/dot_general | solution.py:72
  189.4 5.2 %dynamic_update_slice.10 = f32[1024,4,128]{2,0,1:T(8,128)} dynamic-update-slice(f32[1024,4,128]{2,0,1:T(8,128)} %get-tuple-element.562, f32[512,4,128]{2,0,1:T(8,128)S(1)} %fusion.76, s32[]{:T(128)S(6)} %select_n.158, s32[]{:T(128)} %constant.75.clone.1..sunk.1, s32[]{:T(128)} %constant.75.clone.1..sunk.1) | dynamic-update-slice | bytes 2097156 | tf_op jit(solution)/shard_map/while/body/eval_jaxpr/dynamic_update_slice | solution.py:176
  194.6 5.5 %dynamic_update_slice.11 = f32[1024,4,128]{2,0,1:T(8,128)} dynamic-update-slice(f32[1024,4,128]{2,0,1:T(8,128)} %get-tuple-element.563, f32[512,4,128]{2,0,1:T(8,128)} %fusion.77, s32[]{:T(128)S(6)} %select_n.158, s32[]{:T(128)} %constant.75.clone.1..sunk.1, s32[]{:T(128)} %constant.75.clone.1..sunk.1) | dynamic-update-slice | bytes 2097156 | tf_op jit(solution)/shard_map/while/body/eval_jaxpr/dynamic_update_slice | solution.py:178
  201.4 40.0 %psum.7 = f32[]{:T(128)} all-reduce(f32[]{:T(128)} %convert_reduce_fusion.4), channel_id=1, replica_groups=mesh['grp'=4,'ctx'=8] {'grp','ctx'}, use_global_device_ids=true, to_apply=%region_17.19 | all-reduce | flops 1 | bytes 8 | tf_op jit(solution)/shard_map/psum | solution.py:97
  242.0 1.9 multiply_convert_fusion
  245.2 22.4 %reduce-scatter.5.cloned.1.call-done = f32[128,4,128]{2,0,1:T(8,128)} async-done(((f32[1024,4,128]{2,0,1:T(8,128)}), f32[128,4,128]{2,0,1:T(8,128)}) %reduce-scatter.5.cloned.1.call-update) | async-done | bytes 262160 | tf_op jit(solution)/shard_map/reduce_scatter | solution.py:191
  267.6 70.6 %reduce-scatter.3.cloned.1.call-done = f32[128,4,128]{2,0,1:T(8,128)} async-done(((f32[1024,4,128]{2,0,1:T(8,128)}), f32[128,4,128]{2,0,1:T(8,128)}) %reduce-scatter.3.cloned.1.call-update) | async-done | bytes 262160 | tf_op jit(solution)/shard_map/reduce_scatter | solution.py:190
  (123 shorter events, 46.6 us)
Async XLA Ops:
  7.2 50.1 %copy-start.4 = (s32[1,128]{1,0:T(1,128)S(1)}, s32[1,128]{1,0:T(1,128)}, u32[]{:S(2)}) copy-start(s32[1,128]{1,0:T(1,128)} %param.21) | copy-start | bytes 1540
  7.2 49.9 %copy-start.3 = (s32[1,12]{1,0:T(1,128)S(1)}, s32[1,12]{1,0:T(1,128)}, u32[]{:S(2)}) copy-start(s32[1,12]{1,0:T(1,128)} %param.20) | copy-start | bytes 148
  14.8 37.2 %all-to-all-start = ((bf16[16,8,4096]{2,1,0:T(8,128)(2,1)}), bf16[16,8,4096]{2,1,0:T(8,128)(2,1)S(1)}, u32[]{:S(2)}, u32[]{:S(2)}) async-start(bf16[16,8,4096]{2,1,0:T(8,128)(2,1)} %scatter_fusion), calls=%async_computation | async-start | bytes 2097152 | tf_op jit(solution)/shard_map/all_to_all | solution.py:123
  22.1 64.3 %all-gather.3.cloned.1.call-start = ((), (), s32[]{:S(2)}) async-start(), calls=%async_computation.5 | async-start | bytes 1179648 | tf_op jit(solution)/shard_map/all_gather | solution.py:185
  52.0 38.1 %all-to-all-start.1 = ((bf16[16,8,4096]{2,1,0:T(8,128)(2,1)}), bf16[16,8,4096]{2,1,0:T(8,128)(2,1)}, u32[]{:S(2)}, u32[]{:S(2)}) async-start(bf16[16,8,4096]{2,1,0:T(8,128)(2,1)} %scatter_fusion.1), calls=%async_computation.1 | async-start | bytes 2097152 | tf_op jit(solution)/shard_map/all_to_all | solution.py:124
  56.3 81.5 %all-gather.5.cloned.1.call-start = ((), (), s32[]{:S(2)}) async-start(), calls=%async_computation.6 | async-start | bytes 1179648 | tf_op jit(solution)/shard_map/all_gather | solution.py:186
  90.1 39.3 %all-to-all-start.2 = ((bf16[16,8,4096]{2,1,0:T(8,128)(2,1)}), bf16[16,8,4096]{2,1,0:T(8,128)(2,1)}, u32[]{:S(2)}, u32[]{:S(2)}) async-start(bf16[16,8,4096]{2,1,0:T(8,128)(2,1)} %scatter_fusion.2), calls=%async_computation.2 | async-start | bytes 2097152 | tf_op jit(solution)/shard_map/all_to_all | solution.py:125
  94.3 173.3 %reduce-scatter.5.cloned.1.call-start = ((), (), s32[]{:S(2)}) async-start(), calls=%async_computation.8 | async-start | bytes 2359296 | tf_op jit(solution)/shard_map/reduce_scatter | solution.py:191
  140.7 60.0 %copy-start.5 = (s32[1,128]{1,0:T(1,128)S(1)}, s32[1,128]{1,0:T(1,128)}, u32[]{:S(2)}) copy-start(s32[1,128]{1,0:T(1,128)} %param.19) | copy-start | bytes 1540
  146.2 1.6 copy-start.1
  146.2 1.8 copy-start.2
  151.1 3.6 %copy-start = (f32[1024,4,128]{2,0,1:T(8,128)S(1)}, f32[1024,4,128]{2,0,1:T(8,128)}, u32[]{:S(2)}) copy-start(f32[1024,4,128]{2,0,1:T(8,128)} %get-tuple-element.562) | copy-start | bytes 6291460 | tf_op jit(solution)/shard_map/while
  175.8 1.6 copy-start.1
  175.8 1.8 copy-start.2
  180.7 3.6 %copy-start = (f32[1024,4,128]{2,0,1:T(8,128)S(1)}, f32[1024,4,128]{2,0,1:T(8,128)}, u32[]{:S(2)}) copy-start(f32[1024,4,128]{2,0,1:T(8,128)} %get-tuple-element.562) | copy-start | bytes 6291460 | tf_op jit(solution)/shard_map/while
  200.2 138.1 %reduce-scatter.3.cloned.1.call-start = ((), (), s32[]{:S(2)}) async-start(), calls=%async_computation.7 | async-start | bytes 2359296 | tf_op jit(solution)/shard_map/reduce_scatter | solution.py:190
Sparse Core Ops, SparseCore 0:
  25.0 61.2 all-gather.2
  88.5 45.8 all-gather.4
  200.3 67.3 reduce-scatter.4
  271.0 67.1 reduce-scatter.2
where the time goes:
time: 349 us; the launch traced here: 347 us
  waiting for transfers between devices  158 us (45%)
  local copies, waits for them, and re-layouts  62.7 us (18%)
  blocking collectives  40 us (11%)
  matrix products  27.4 us (8%)
  other arithmetic  21.9 us (6%)
  starting transfers between devices  15.9 us (5%)
  between operations  14.7 us (4%)
  loops' own time  6.75 us (2%)
    reduce_scatter x1, waiting for transfers between devices, shards(): lax.psum_scatter(dk_all, 'ctx', scatter_dimension=0, tiled=True)  70.6 us
    psum x1, blocking collectives, shards(): total_counted = lax.psum(counted, ('grp', 'ctx'))  40 us
    all_to_all x1, waiting for transfers between devices, shards(): lax.all_to_all(pack_rows(query_rows[0]), 'ctx', split_axis=0, concat_axis...  23 us
    reduce_scatter x1, waiting for transfers between devices, shards(): lax.psum_scatter(dv_all, 'ctx', scatter_dimension=0, tiled=True)  22.4 us
    all_gather x1, waiting for transfers between devices, shards(): lax.all_gather(key_rows, 'ctx', axis=1, tiled=True)[0]  21 us
    all_to_all x1, waiting for transfers between devices, shards(): lax.all_to_all(pack_rows(output_rows[0]), 'ctx', split_axis=0, concat_axi...  17.6 us
    dynamic_update_slice x2, local copies, waits for them, and re-layouts, grads_step_rows(): lax.dynamic_update_slice_in_dim(dv_all, old_values + value_part, first_ro...  11.7 us
    dynamic_update_slice x2, local copies, waits for them, and re-layouts, grads_step_rows(): lax.dynamic_update_slice_in_dim(dk_all, old_keys + key_part, first_row, 0)  11.1 us
  transfers between devices with their start and end apart: 7, of which 6 were waited for; matrix products, arithmetic and copies ran while one was open for 13% of the time, Pallas kernels for 0%

commit v1 on v0

--- a/solution.py
+++ b/solution.py
@@ -1,3 +1,4 @@
+import functools
 import jax
 import jax.numpy as jnp
 from jax import lax
@@ -8,6 +9,36 @@
 KVH = 4
 SPAN = 8
 NEGATIVE = -1e30
+
+
+def build_routes_all_here(local, dim_at):
+    local = jnp.moveaxis(local, 0, dim_at)
+    u_next = local.shape
+    return local.reshape(
+        *u_next[:dim_at], u_next[dim_at] * u_next[dim_at + 1], *u_next[dim_at + 2 :]
+    )
+
+
+def proceed_the_column(matrix, group_axis):
+    num = lax.axis_size(group_axis)
+    seen_now = matrix[None]
+    for ix in range(num.bit_length() - 1):
+        ready = 1 << ix
+        column = []
+        for k in range(num):
+            column.append((k, k ^ ready))
+        s_next = lax.ppermute(seen_now, axis_name=group_axis, perm=column)
+        out_arr = jnp.stack([seen_now, s_next], 0)
+        current_arr = lax.axis_index(group_axis) >> ix & 1
+        seen_now = jnp.where(current_arr == 0, out_arr, out_arr[::-1]).reshape(-1, *matrix.shape)
+    return seen_now
+
+
+def load_the_strings(frame_in, mine_x, at_axis):
+    return build_routes_all_here(proceed_the_column(frame_in, mine_x), at_axis)
+
+
+launch_frame = functools.partial(load_the_strings, mine_x="ctx", at_axis=1)
 
 
 def key_block():
@@ -181,10 +212,7 @@
     dq_sum, dk_all, dv_all = over_blocks(
         grads_step_rows,
         grads_initial,
-        (
-            lax.all_gather(key_rows, "ctx", axis=1, tiled=True)[0],
-            lax.all_gather(value_rows, "ctx", axis=1, tiled=True)[0],
-        ),
+        (launch_frame(key_rows)[0], lax.all_gather(value_rows, "ctx", axis=1, tiled=True)[0]),
     )
     dk_mine, dv_mine = (
         lax.psum_scatter(dk_all, "ctx", scatter_dimension=0, tiled=True),

time: 349 us -> 375 us (1.074)
  waiting for transfers between devices: 158 us -> 176 us
  starting transfers between devices: 15.9 us -> 24 us
    ppermute x0 -> x3, waiting for transfers between devices: none -> 48.1 us  [proceed_the_column(): s_next = lax.ppermute(seen_now, axis_name=group_axis, perm=column)]
    all_gather x1, waiting for transfers between devices: 21 us -> 0.02 us  [shards(): lax.all_gather(key_rows, 'ctx', axis=1, tiled=True)[0]]
    all_to_all x1, waiting for transfers between devices: 17.6 us -> 5.58 us  [shards(): lax.all_to_all(pack_rows(output_rows[0]), 'ctx', split_axis=0, concat_axi...]
    ppermute x0 -> x3, starting transfers between devices: none -> 8.58 us  [proceed_the_column(): s_next = lax.ppermute(seen_now, axis_name=group_axis, perm=column)]
    dynamic_slice x12 -> x14, local copies, waits for them, and re-layouts: 5.12 us -> 10.1 us  [over_blocks(): lax.scan(advance, folded, (jnp.arange(step_count, dtype=jnp.int32), stack...]
    another operation x5 -> x7, local copies, waits for them, and re-layouts: 6.16 us -> 8.49 us
  transfers between devices with their start and end apart: 7 -> 10, of which waited for: 6 -> 6; matrix products, arithmetic and copies ran while one was open for 13% -> 15% of each run, Pallas kernels for 0% -> 0%
where the time goes in v1:
time: 375 us; the launch traced here: 373 us
  waiting for transfers between devices  176 us (47%)
  local copies, waits for them, and re-layouts  65.8 us (18%)
  blocking collectives  38.4 us (10%)
  matrix products  25.5 us (7%)
  starting transfers between devices  24 us (6%)
  other arithmetic  21.8 us (6%)
  between operations  14.8 us (4%)
  loops' own time  6.95 us (2%)
    reduce_scatter x1, waiting for transfers between devices, shards(): lax.psum_scatter(dk_all, 'ctx', scatter_dimension=0, tiled=True)  70.6 us
    ppermute x3, waiting for transfers between devices, proceed_the_column(): s_next = lax.ppermute(seen_now, axis_name=group_axis, perm=column)  48.1 us
    psum x1, blocking collectives, shards(): total_counted = lax.psum(counted, ('grp', 'ctx'))  38.4 us
    all_to_all x1, waiting for transfers between devices, shards(): lax.all_to_all(pack_rows(query_rows[0]), 'ctx', split_axis=0, concat_axis...  26.3 us
    reduce_scatter x1, waiting for transfers between devices, shards(): lax.psum_scatter(dv_all, 'ctx', scatter_dimension=0, tiled=True)  24.1 us
    dynamic_update_slice x2, local copies, waits for them, and re-layouts, grads_step_rows(): lax.dynamic_update_slice_in_dim(dk_all, old_keys + key_part, first_row, 0)  11.1 us
    dynamic_update_slice x2, local copies, waits for them, and re-layouts, grads_step_rows(): lax.dynamic_update_slice_in_dim(dv_all, old_values + value_part, first_ro...  11.1 us
    dynamic_slice x14, local copies, waits for them, and re-layouts, over_blocks(): lax.scan(advance, folded, (jnp.arange(step_count, dtype=jnp.int32), stack...  10.1 us
  transfers between devices with their start and end apart: 10, of which 6 were waited for; matrix products, arithmetic and copies ran while one was open for 15% of the time, Pallas kernels for 0%

profile of v1, /device:TPU:0, one launch (start us, length us, event | category | flops | bytes accessed | tf_op | source)
XLA Modules:
  0.0 373.2 jit_solution(17545075769265312705)
XLA Ops:
  12.1 3.4 scatter_fusion
  15.4 7.3 %all-to-all-start = ((bf16[16,8,4096]{2,1,0:T(8,128)(2,1)}), bf16[16,8,4096]{2,1,0:T(8,128)(2,1)S(1)}, u32[]{:S(2)}, u32[]{:S(2)}) async-start(bf16[16,8,4096]{2,1,0:T(8,128)(2,1)} %scatter_fusion), calls=%async_computation | async-start | bytes 2097152 | tf_op jit(solution)/shard_map/all_to_all | solution.py:154
  22.7 2.0 collective-permute-start
  26.9 2.5 sort.17
  30.6 3.0 scatter_fusion.1
  33.6 26.3 %all-to-all-done = bf16[16,8,4096]{2,1,0:T(8,128)(2,1)S(1)} async-done(((bf16[16,8,4096]{2,1,0:T(8,128)(2,1)}), bf16[16,8,4096]{2,1,0:T(8,128)(2,1)S(1)}, u32[]{:S(2)}, u32[]{:S(2)}) %all-to-all-start) | async-done | bytes 1048608 | tf_op jit(solution)/shard_map/all_to_all | solution.py:154
  59.9 3.6 all-to-all-start.1
  63.5 2.0 collective-permute-start.1
  65.9 24.3 %collective-permute-done.1 = bf16[2,1,128,512]{3,2,0,1:T(8,128)(2,1)S(1)} collective-permute-done((bf16[2,1,128,512]{3,2,0,1:T(8,128)(2,1)S(1)}, bf16[2,1,128,512]{3,2,0,1:T(8,128)(2,1)S(1)}, u32[]{:S(2)}, u32[]{:S(2)}) %collective-permute-start.1) | collective-permute-done | bytes 262176 | tf_op jit(solution)/shard_map/ppermute | solution.py:30
  91.4 4.6 %collective-permute-start.2 = (bf16[4,1,128,512]{2,0,3,1:T(4,128)(2,1)}, bf16[4,1,128,512]{2,0,3,1:T(4,128)(2,1)}, u32[]{:S(2)}, u32[]{:S(2)}) collective-permute-start(bf16[4,1,128,512]{2,0,3,1:T(4,128)(2,1)} %copy.62), channel_id=1, source_target_pairs={{0,4},{1,5},{2,6},{3,7},{4,0},{5,1},{6,2},{7,3},{8,12},{9,13},{10,... | collective-permute-start | bytes 1572872 | tf_op jit(solution)/shard_map/ppermute | solution.py:30
  97.9 3.4 scatter_fusion.2
  102.6 23.8 %collective-permute-done.2 = bf16[4,1,128,512]{2,0,3,1:T(4,128)(2,1)} collective-permute-done((bf16[4,1,128,512]{2,0,3,1:T(4,128)(2,1)}, bf16[4,1,128,512]{2,0,3,1:T(4,128)(2,1)}, u32[]{:S(2)}, u32[]{:S(2)}) %collective-permute-start.2) | collective-permute-done | bytes 524320 | tf_op jit(solution)/shard_map/ppermute | solution.py:30
  126.4 2.0 pad_maximum_fusion
  130.7 4.3 %all-to-all-start.2 = ((bf16[16,8,4096]{2,1,0:T(8,128)(2,1)}), bf16[16,8,4096]{2,1,0:T(8,128)(2,1)}, u32[]{:S(2)}, u32[]{:S(2)}) async-start(bf16[16,8,4096]{2,1,0:T(8,128)(2,1)} %scatter_fusion.2), calls=%async_computation.2 | async-start | bytes 2097152 | tf_op jit(solution)/shard_map/all_to_all | solution.py:156
  138.9 13.6 %while.28 = (s32[]{:T(128)}, f32[4,8,128]{2,1,0:T(8,128)S(1)}, f32[4,8,128]{2,1,0:T(8,128)S(1)}, s32[2]{0:T(128)S(1)}, s32[12]{0:T(128)S(1)}, /*index=5*/s32[128...) while((s32[]{:T(128)}, f32[4,8,128]{2,1,0:T(8,128)S(1)}, ...), condition=%wide.region_9.11_spmd.clone, body=%wide.region_5.10_spmd.clone.sunk | while | flops 553883776 | bytes 20869912 | solution.py:77
  143.6 2.2 select_reduce_fusion.2
  150.4 2.2 select_reduce_fusion.2
  155.4 5.6 %all-to-all-done.2 = bf16[16,8,4096]{2,1,0:T(8,128)(2,1)} async-done(((bf16[16,8,4096]{2,1,0:T(8,128)(2,1)}), bf16[16,8,4096]{2,1,0:T(8,128)(2,1)}, u32[]{:S(2)}, u32[]{:S(2)}) %all-to-all-start.2) | async-done | bytes 1048608 | tf_op jit(solution)/shard_map/all_to_all | solution.py:156
  167.3 58.4 %while.29 = (s32[]{:T(128)}, f32[128,4,8,128]{0,3,2,1:T(8,128)}, f32[1024,4,128]{2,0,1:T(8,128)}, f32[1024,4,128]{2,0,1:T(8,128)}, bf16[2,512,512]{1,2,0:T(8,128...) while((s32[]{:T(128)}, f32[128,4,8,128]{0,3,2,1:T(8,128)}, ...), condition=%wide.region_15.17_spmd.clone, body=%wide.region_13.16_spmd.clone.sunk | while | flops 2713405440 | bytes 80475096 | solution.py:77
  175.3 2.1 fusion.79
  177.4 3.6 fusion.77
  182.3 2.3 bitcast_add_fusion.2
  184.6 5.9 %dynamic_update_slice.10 = f32[1024,4,128]{2,0,1:T(8,128)} dynamic-update-slice(f32[1024,4,128]{2,0,1:T(8,128)} %get-tuple-element.564, f32[512,4,128]{2,0,1:T(8,128)S(1)} %fusion.78, s32[]{:T(128)S(6)} %select_n.202, s32[]{:T(128)} %constant.75.clone.1..sunk.1, s32[]{:T(128)} %constant.75.clone.1..sunk.1) | dynamic-update-slice | bytes 2097156 | tf_op jit(solution)/shard_map/while/body/eval_jaxpr/dynamic_update_slice | solution.py:207
  190.5 5.9 %dynamic_update_slice.11 = f32[1024,4,128]{2,0,1:T(8,128)} dynamic-update-slice(f32[1024,4,128]{2,0,1:T(8,128)} %get-tuple-element.565, f32[512,4,128]{2,0,1:T(8,128)S(1)} %fusion.79, s32[]{:T(128)S(6)} %select_n.202, s32[]{:T(128)} %constant.75.clone.1..sunk.1, s32[]{:T(128)} %constant.75.clone.1..sunk.1) | dynamic-update-slice | bytes 2097156 | tf_op jit(solution)/shard_map/while/body/eval_jaxpr/dynamic_update_slice | solution.py:209
  204.4 2.1 fusion.79
  206.5 3.6 fusion.77
  211.4 3.9 %bitcast_add_fusion.2 = f32[128,4,8,128]{0,3,2,1:T(8,128)} fusion(f32[128,4,8,128]{0,3,2,1:T(8,128)} %get-tuple-element.563, bf16[512,4,128,1]{0,2,3,1:T(8,128)(2,1)S(1)} %bitcast.175, bf16[4,8,128,512]{2,3,1,0:T(8,128)(2,1)S(1)} %fusion.77, pred[]{:T(512)S(6)} %compare.25), kind=kOutput, calls=%fused_computation.31.clone.1 | convolution fusion | flops 537919488 | bytes 8912897 | tf_op jit(solution)/shard_map/while/body/eval_jaxpr/gsrn,ngd->rgsd/dot_general | solution.py:103
  215.3 5.2 %dynamic_update_slice.10 = f32[1024,4,128]{2,0,1:T(8,128)} dynamic-update-slice(f32[1024,4,128]{2,0,1:T(8,128)} %get-tuple-element.564, f32[512,4,128]{2,0,1:T(8,128)S(1)} %fusion.78, s32[]{:T(128)S(6)} %select_n.202, s32[]{:T(128)} %constant.75.clone.1..sunk.1, s32[]{:T(128)} %constant.75.clone.1..sunk.1) | dynamic-update-slice | bytes 2097156 | tf_op jit(solution)/shard_map/while/body/eval_jaxpr/dynamic_update_slice | solution.py:207
  220.5 5.2 %dynamic_update_slice.11 = f32[1024,4,128]{2,0,1:T(8,128)} dynamic-update-slice(f32[1024,4,128]{2,0,1:T(8,128)} %get-tuple-element.565, f32[512,4,128]{2,0,1:T(8,128)S(1)} %fusion.79, s32[]{:T(128)S(6)} %select_n.202, s32[]{:T(128)} %constant.75.clone.1..sunk.1, s32[]{:T(128)} %constant.75.clone.1..sunk.1) | dynamic-update-slice | bytes 2097156 | tf_op jit(solution)/shard_map/while/body/eval_jaxpr/dynamic_update_slice | solution.py:209
  226.9 38.4 %psum.7 = f32[]{:T(128)} all-reduce(f32[]{:T(128)} %convert_reduce_fusion.4), channel_id=1, replica_groups=mesh['grp'=4,'ctx'=8] {'grp','ctx'}, use_global_device_ids=true, to_apply=%region_17.19 | all-reduce | flops 1 | bytes 8 | tf_op jit(solution)/shard_map/psum | solution.py:128
  269.2 24.1 %reduce-scatter.5.cloned.1.call-done = f32[128,4,128]{2,0,1:T(8,128)} async-done(((f32[1024,4,128]{2,0,1:T(8,128)}), f32[128,4,128]{2,0,1:T(8,128)}) %reduce-scatter.5.cloned.1.call-update) | async-done | bytes 262160 | tf_op jit(solution)/shard_map/reduce_scatter | solution.py:219
  293.4 70.6 %reduce-scatter.3.cloned.1.call-done = f32[128,4,128]{2,0,1:T(8,128)} async-done(((f32[1024,4,128]{2,0,1:T(8,128)}), f32[128,4,128]{2,0,1:T(8,128)}) %reduce-scatter.3.cloned.1.call-update) | async-done | bytes 262160 | tf_op jit(solution)/shard_map/reduce_scatter | solution.py:218
  (143 shorter events, 56.4 us)
Async XLA Ops:
  7.2 26.4 %copy-start.4 = (bf16[1,128,512]{2,1,0:T(8,128)(2,1)S(1)}, bf16[1,128,512]{2,1,0:T(8,128)(2,1)}, u32[]{:S(2)}) copy-start(bf16[1,128,512]{2,1,0:T(8,128)(2,1)} %param.15) | copy-start | bytes 393220
  7.2 19.8 %copy-start.5 = (s32[1,128]{1,0:T(1,128)S(1)}, s32[1,128]{1,0:T(1,128)}, u32[]{:S(2)}) copy-start(s32[1,128]{1,0:T(1,128)} %param.21) | copy-start | bytes 1540
  7.2 58.4 %copy-start.6 = (s32[1,12]{1,0:T(1,128)S(1)}, s32[1,12]{1,0:T(1,128)}, u32[]{:S(2)}) copy-start(s32[1,12]{1,0:T(1,128)} %param.20) | copy-start | bytes 148
  7.2 131.7 %all-gather.3.cloned.1.call-start = ((), (), s32[]{:S(2)}) async-start(), calls=%async_computation.5 | async-start | bytes 1179648 | tf_op jit(solution)/shard_map/all_gather | solution.py:179
  15.4 44.5 %all-to-all-start = ((bf16[16,8,4096]{2,1,0:T(8,128)(2,1)}), bf16[16,8,4096]{2,1,0:T(8,128)(2,1)S(1)}, u32[]{:S(2)}, u32[]{:S(2)}) async-start(bf16[16,8,4096]{2,1,0:T(8,128)(2,1)} %scatter_fusion), calls=%async_computation | async-start | bytes 2097152 | tf_op jit(solution)/shard_map/all_to_all | solution.py:154
  22.7 141.7 %all-gather.5.cloned.1.call-start = ((), (), s32[]{:S(2)}) async-start(), calls=%async_computation.6 | async-start | bytes 1179648 | tf_op jit(solution)/shard_map/all_gather | solution.py:215
  22.7 10.8 %collective-permute-start = (bf16[1,1,128,512]{3,2,1,0:T(8,128)(2,1)}, bf16[1,1,128,512]{3,2,1,0:T(8,128)(2,1)S(1)}, u32[]{:S(2)}, u32[]{:S(2)}) collective-permute-start(bf16[1,1,128,512]{3,2,1,0:T(8,128)(2,1)} %bitcast.188), channel_id=1, source_target_pairs={{0,1},{1,0},{2,3},{3,2},{4,5},{5,4},{6,7},{7,6},{8,9},{9,8},{10,11... | collective-permute-start | bytes 393224 | tf_op jit(solution)/shard_map/ppermute | solution.py:30
  59.9 70.7 %all-to-all-start.1 = ((bf16[16,8,4096]{2,1,0:T(8,128)(2,1)}), bf16[16,8,4096]{2,1,0:T(8,128)(2,1)S(1)}, u32[]{:S(2)}, u32[]{:S(2)}) async-start(bf16[16,8,4096]{2,1,0:T(8,128)(2,1)} %scatter_fusion.1), calls=%async_computation.1 | async-start | bytes 2097152 | tf_op jit(solution)/shard_map/all_to_all | solution.py:155
  63.5 26.6 %collective-permute-start.1 = (bf16[2,1,128,512]{3,2,0,1:T(8,128)(2,1)S(1)}, bf16[2,1,128,512]{3,2,0,1:T(8,128)(2,1)S(1)}, u32[]{:S(2)}, u32[]{:S(2)}) collective-permute-start(bf16[2,1,128,512]{3,2,0,1:T(8,128)(2,1)S(1)} %get-tuple-element.357), channel_id=1, source_target_pairs={{0,2},{1,3},{2,0},{3,1},{4,6},{5,7},{6,4},{7,5},{8,10},{9,11},{10,... | collective-permute-start | bytes 786440 | tf_op jit(solution)/shard_map/ppermute | solution.py:30
  91.4 35.0 %collective-permute-start.2 = (bf16[4,1,128,512]{2,0,3,1:T(4,128)(2,1)}, bf16[4,1,128,512]{2,0,3,1:T(4,128)(2,1)}, u32[]{:S(2)}, u32[]{:S(2)}) collective-permute-start(bf16[4,1,128,512]{2,0,3,1:T(4,128)(2,1)} %copy.62), channel_id=1, source_target_pairs={{0,4},{1,5},{2,6},{3,7},{4,0},{5,1},{6,2},{7,3},{8,12},{9,13},{10,... | collective-permute-start | bytes 1572872 | tf_op jit(solution)/shard_map/ppermute | solution.py:30
  130.6 4.3 %copy-start.2 = (bf16[16,8,4096]{2,1,0:T(8,128)(2,1)}, bf16[16,8,4096]{2,1,0:T(8,128)(2,1)S(1)}, u32[]{:S(2)}) copy-start(bf16[16,8,4096]{2,1,0:T(8,128)(2,1)S(1)} %all-to-all-done.1) | copy-start | bytes 3145732
  130.7 30.3 %all-to-all-start.2 = ((bf16[16,8,4096]{2,1,0:T(8,128)(2,1)}), bf16[16,8,4096]{2,1,0:T(8,128)(2,1)}, u32[]{:S(2)}, u32[]{:S(2)}) async-start(bf16[16,8,4096]{2,1,0:T(8,128)(2,1)} %scatter_fusion.2), calls=%async_computation.2 | async-start | bytes 2097152 | tf_op jit(solution)/shard_map/all_to_all | solution.py:156
  134.9 158.4 %reduce-scatter.5.cloned.1.call-start = ((), (), s32[]{:S(2)}) async-start(), calls=%async_computation.8 | async-start | bytes 2359296 | tf_op jit(solution)/shard_map/reduce_scatter | solution.py:219
  167.3 59.0 %copy-start.7 = (s32[1,128]{1,0:T(1,128)S(1)}, s32[1,128]{1,0:T(1,128)}, u32[]{:S(2)}) copy-start(s32[1,128]{1,0:T(1,128)} %param.19) | copy-start | bytes 1540
  172.8 2.6 copy-start.1
  172.8 2.6 copy-start.3
  177.4 3.6 copy-start
  201.9 2.6 copy-start.1
  201.9 2.6 copy-start.3
  206.5 3.6 copy-start
  225.7 138.3 %reduce-scatter.3.cloned.1.call-start = ((), (), s32[]{:S(2)}) async-start(), calls=%async_computation.7 | async-start | bytes 2359296 | tf_op jit(solution)/shard_map/reduce_scatter | solution.py:218
Sparse Core Ops, SparseCore 0:
  10.2 50.5 all-gather.2
  62.9 56.6 all-gather.4
  225.8 67.5 reduce-scatter.4
  296.8 67.1 reduce-scatter.2
